TPU v7x, 512 devices: a whole 4x4x16 slice. The times are simulated.
512 devices in a mesh: seq: 64 (over z, y_lo, core), kv: 8 (over y_hi, x).
Axes of the slice: x: 4, y: 4 (y_hi: 2, y_lo: 2; y = y_hi * 2 + y_lo), z: 16, core: 2. Of those that a mesh axis runs over, the one named last changes fastest.
Arguments:
- queries: bfloat16 [8192, 8192], P('seq', 'kv'), parts along dimension 1, may hold values from -4.5 to 4.5
- keys: bfloat16 [8192, 1024], P('seq', 'kv'), parts along dimension 1, may hold values from -4.5 to 4.5
- values: bfloat16 [8192, 1024], P('seq', 'kv'), parts along dimension 1, may hold values from -6 to 6
- block_order: int32 [128], replicated, may hold values from 0 to 127, each once
Outputs:
- attention: bfloat16 [8192, 8192], P('seq', 'kv'), parts along dimension 1
- row_lse: float32 [64, 8192], P('kv', 'seq'), parts along dimension 0
- column_sums: float32 [65536], P(('kv', 'seq')), parts along dimension 0
There are 8 independent parts, one for each index of `kv`. A program takes and returns all parts, laid end to end along the dimension named above; an argument that names none is the same for every part. Nothing has to cross between parts.
Inputs may be any that keep to these rules, and one draw needn't show every extreme that they name: `block_order`: every value of 0 to 127 appears once.
All inputs are finite; a program needn't handle non-finite values.
Results may differ from a plain program's by a relative error of at most 0.0047.
Values may be sent and summed in bfloat16 or wider, within the bound.
A program may use at most 64 MiB of HBM per device.

v0:
```python
import math
import jax
import jax.numpy as jnp
from jax import lax
from jax.sharding import PartitionSpec as P

BLOCK = 64
NEG_FILL = -1e30


def key_positions(block_order, first_row, count):
    row_ids = first_row + jnp.arange(count, dtype=jnp.int32)
    block_ids = row_ids // BLOCK
    one_hot = block_ids[:, None] == jnp.arange(block_order.shape[0], dtype=jnp.int32)[None, :]
    chosen = jnp.sum(jnp.where(one_hot, block_order[None, :], 0), axis=1)
    return chosen * BLOCK + row_ids % BLOCK


def tile_scores(query_heads, key_tile, query_pos, key_pos):
    factor = 1.0 / math.sqrt(key_tile.shape[1])
    scaled = (
        jnp.einsum("qhd,kd->hqk", query_heads, key_tile, preferred_element_type=jnp.float32)
        * factor
    )
    allowed = key_pos[None, :] <= query_pos[:, None]
    return jnp.where(allowed[None, :, :], scaled, NEG_FILL)


def over_tiles(update, carried, key_arrays, first_row, block_order):
    count = key_arrays[0].shape[0]
    width = math.gcd(count, 512)
    turns = count // width

    def one_turn(turn_index, running):
        offset = turn_index * width
        tiles = tuple((lax.dynamic_slice_in_dim(member, offset, width, 0) for member in key_arrays))
        key_pos = key_positions(block_order, first_row + offset, width)
        return update(running, tiles, key_pos, first_row + offset)

    return lax.fori_loop(0, turns, one_turn, carried)


def local(queries, keys, values, block_order):
    tok_rows = queries.shape[0]
    head_dim = keys.shape[1]
    head_count = queries.shape[1] // head_dim
    query_heads = queries.reshape(tok_rows, head_count, head_dim)
    own_first = lax.axis_index("seq") * tok_rows
    query_pos = key_positions(block_order, own_first, tok_rows)
    all_rows = tok_rows * lax.axis_size("seq")

    def stats_update(running, tiles, key_pos, first_row):
        top, total = running
        scores = tile_scores(query_heads, tiles[0], query_pos, key_pos)
        new_top = jnp.maximum(top, jnp.max(scores, axis=2))
        total = total * jnp.exp(top - new_top) + jnp.sum(
            jnp.exp(scores - new_top[:, :, None]), axis=2
        )
        return (new_top, total)

    def make_mix(row_lse):

        def mix_update(running, tiles, key_pos, first_row):
            accum, columns = running
            scores = tile_scores(query_heads, tiles[0], query_pos, key_pos)
            probs = jnp.exp(scores - row_lse[:, :, None])
            columns = lax.dynamic_update_slice_in_dim(
                columns, jnp.sum(probs, axis=(0, 1)), first_row, 0
            )
            accum = accum + jnp.einsum(
                "hqk,kd->qhd",
                probs.astype(jnp.bfloat16),
                tiles[1],
                preferred_element_type=jnp.float32,
            )
            return (accum, columns)

        return mix_update

    init_stats = (
        jnp.full((head_count, tok_rows), NEG_FILL, jnp.float32),
        jnp.zeros((head_count, tok_rows), jnp.float32),
    )
    init_mix = (
        jnp.zeros((tok_rows, head_count, head_dim), jnp.float32),
        jnp.zeros((all_rows,), jnp.float32),
    )
    whole_keys, whole_values = (
        lax.all_gather(keys, "seq", axis=0, tiled=True),
        lax.all_gather(values, "seq", axis=0, tiled=True),
    )
    top, total = over_tiles(stats_update, init_stats, (whole_keys,), 0, block_order)
    row_lse = top + jnp.log(total)
    accum, columns = over_tiles(
        make_mix(row_lse), init_mix, (whole_keys, whole_values), 0, block_order
    )
    attention = accum.reshape(tok_rows, head_count * head_dim).astype(jnp.bfloat16)
    column_sums = lax.psum_scatter(columns, "seq", scatter_dimension=0, tiled=True)
    return (attention, row_lse, column_sums)


def solution(mesh):
    placed = (P("seq", "kv"), P("seq", "kv"), P("seq", "kv"), P())
    return jax.shard_map(
        local,
        mesh=mesh,
        in_specs=placed,
        out_specs=(P("seq", "kv"), P("kv", "seq"), P(("kv", "seq"))),
        check_vma=False,
    )
```

profile of v0, /device:TPU:2, one launch (start us, length us, event | category | flops | bytes accessed | tf_op | source)
XLA Modules:
  0.0 545.5 jit_solution(4366825946389751583)
XLA Ops:
  7.9 1.5 copy.19
  13.6 123.1 %all-gather.5.cloned.1.call-done = bf16[8192,128]{1,0:T(8,128)(2,1)} async-done(((bf16[128,128]{1,0:T(8,128)(2,1)}), bf16[8192,128]{1,0:T(8,128)(2,1)}) %all-gather.5.cloned.1.call-update) | async-done | bytes 2097168 | tf_op jit(solution)/shard_map/all_gather | solution.py:89
  136.7 47.2 %while.36 = (s32[]{:T(128)}, f32[8,128]{1,0:T(8,128)S(1)}, f32[8,128]{1,0:T(8,128)S(1)}, s32[128]{0:T(128)}, s32[128]{0:T(128)S(1)}, /*index=5*/bf16[8192,128]{1...) while((s32[]{:T(128)}, f32[8,128]{1,0:T(8,128)S(1)}, ...), condition=%wide.region_5.6_spmd.clone, body=%wide.region_1.5_spmd.clone.sunk | while | flops 138169856 | bytes 4850866 | solution.py:40
  184.0 73.2 %all-gather.3.cloned.1.call-done = bf16[8192,128]{0,1:T(8,128)(2,1)} async-done(((bf16[128,128]{0,1:T(8,128)(2,1)}), bf16[8192,128]{0,1:T(8,128)(2,1)}) %all-gather.3.cloned.1.call-update) | async-done | bytes 2097168 | tf_op jit(solution)/shard_map/all_gather | solution.py:90
  257.1 70.1 %while.37 = (s32[]{:T(128)}, f32[128,8,128]{0,2,1:T(8,128)S(1)}, f32[8192]{0:T(1024)S(1)}, bf16[8192,128]{0,1:T(8,128)(2,1)}, s32[128]{0:T(128)}, /*index=5*/s32...) while((s32[]{:T(128)}, f32[128,8,128]{0,2,1:T(8,128)S(1)}, ...), condition=%wide.region_9.10_spmd.clone, body=%wide.region_6.9_spmd.clone.sunk | while | flops 271595520 | bytes 3824841 | solution.py:40
  258.2 1.6 fusion.47
  262.5 1.6 fusion.47
  264.2 1.4 fusion.48
  266.9 1.6 fusion.47
  268.5 1.4 fusion.48
  271.3 1.6 fusion.47
  272.9 1.4 fusion.48
  275.7 1.6 fusion.47
  277.3 1.4 fusion.48
  280.1 1.6 fusion.47
  281.7 1.4 fusion.48
  284.5 1.6 fusion.47
  286.1 1.4 fusion.48
  288.9 1.6 fusion.47
  290.5 1.4 fusion.48
  293.2 1.6 fusion.47
  297.6 1.6 fusion.47
  299.3 1.4 fusion.48
  302.0 1.6 fusion.47
  306.4 1.6 fusion.47
  310.8 1.6 fusion.47
  312.4 1.4 fusion.48
  315.2 1.6 fusion.47
  319.6 1.6 fusion.47
  321.2 1.4 fusion.48
  323.9 1.6 fusion.47
  328.2 209.9 %all-reduce = f32[8192]{0:T(1024)S(1)} all-reduce(f32[8192]{0:T(1024)S(1)} %get-tuple-element.410), channel_id=2, replica_groups=mesh['seq'=64,'kv'=8] {'seq'}, use_global_device_ids=true, to_apply=%region_10.11.clone | all-reduce | flops 8192 | bytes 65536
  (250 shorter events, 81.1 us)
Async XLA Ops:
  7.2 129.6 %all-gather.5.cloned.1.call-start = ((), (), s32[]{:S(2)}) async-start(), calls=%async_computation.1 | async-start | bytes 2129920 | tf_op jit(solution)/shard_map/all_gather | solution.py:89
  7.9 249.2 %all-gather.3.cloned.1.call-start = ((), (), s32[]{:S(2)}) async-start(), calls=%async_computation | async-start | bytes 2129920 | tf_op jit(solution)/shard_map/all_gather | solution.py:90
  327.3 211.4 %copy-start = (f32[8,128]{1,0:T(8,128)}, f32[8,128]{1,0:T(8,128)S(1)}, u32[]{:S(2)}) copy-start(f32[8,128]{1,0:T(8,128)S(1)} %get-tuple-element.741) | copy-start | bytes 12292
Sparse Core Ops, SparseCore 0:
  10.2 126.5 all-gather.4
  139.4 117.7 all-gather.2
where the time goes:
time: 547 us; the launch traced here: 546 us
  blocking collectives  210 us (38%)
  waiting for transfers between devices  197 us (36%)
  matrix products  70.7 us (13%)
  other arithmetic  41.4 us (8%)
  between operations  14.8 us (3%)
  local copies, waits for them, and re-layouts  9.99 us (2%)
    unnamed x1, blocking collectives  210 us
    all_gather x1, waiting for transfers between devices, local(): lax.all_gather(keys, 'seq', axis=0, tiled=True)  123 us
    all_gather x1, waiting for transfers between devices, local(): lax.all_gather(values, 'seq', axis=0, tiled=True)  73.2 us
    dot_general x32, matrix products, tile_scores(): jnp.einsum('qhd,kd->hqk', query_heads, key_tile, preferred_element_type=j...  47.6 us
    reduce_sum x33, other arithmetic, key_positions(): chosen = jnp.sum(jnp.where(one_hot, block_order[None, :], 0), axis=1)  29.2 us
    dot_general x16, matrix products, mix_update(): jnp.einsum('hqk,kd->qhd', probs.astype(jnp.bfloat16), tiles[1], preferred...  23.1 us
  transfers between devices with their start and end apart: 2, of which 2 were waited for; matrix products, arithmetic and copies ran while one was open for 9% of the time, Pallas kernels for 0%

commit v1 on v0

--- a/solution.py
+++ b/solution.py
@@ -86,7 +86,9 @@
         jnp.zeros((all_rows,), jnp.float32),
     )
     whole_keys, whole_values = (
-        lax.all_gather(keys, "seq", axis=0, tiled=True),
+        jnp.concatenate(
+            lax.all_to_all(jnp.stack([keys] * lax.axis_size("seq")), "seq", 0, 0), axis=0
+        ),
         lax.all_gather(values, "seq", axis=0, tiled=True),
     )
     top, total = over_tiles(stats_update, init_stats, (whole_keys,), 0, block_order)

time: 547 us -> 470 us (0.86)
  the two profiles are of different devices: /device:TPU:2 before, /device:TPU:4 now
where the time goes in v1:
time: 470 us; the launch traced here: 469 us
  blocking collectives  209 us (44%)
  waiting for transfers between devices  124 us (26%)
  matrix products  70.8 us (15%)
  other arithmetic  19.8 us (4%)
  starting transfers between devices  17.5 us (4%)
  between operations  14.7 us (3%)
  local copies, waits for them, and re-layouts  10.9 us (2%)
    unnamed x1, blocking collectives  209 us
    all_to_all x1, waiting for transfers between devices, local(): lax.all_to_all(jnp.stack([keys] * lax.axis_size('seq')), 'seq', 0, 0)  98.6 us
    dot_general x32, matrix products, tile_scores(): jnp.einsum('qhd,kd->hqk', query_heads, key_tile, preferred_element_type=j...  47.7 us
    all_gather x1, waiting for transfers between devices, local(): lax.all_gather(values, 'seq', axis=0, tiled=True)  25.3 us
    dot_general x16, matrix products, mix_update(): jnp.einsum('hqk,kd->qhd', probs.astype(jnp.bfloat16), tiles[1], preferred...  23.1 us
    all_to_all x1, starting transfers between devices, local(): lax.all_to_all(jnp.stack([keys] * lax.axis_size('seq')), 'seq', 0, 0)  17.5 us
  transfers between devices with their start and end apart: 2, of which 2 were waited for; matrix products, arithmetic and copies ran while one was open for 8% of the time, Pallas kernels for 0%

profile of v1, /device:TPU:4, one launch (start us, length us, event | category | flops | bytes accessed | tf_op | source)
XLA Modules:
  0.0 468.7 jit_solution(6222555116387486209)
XLA Ops:
  7.2 2.6 stack.2
  9.8 17.5 %all-to-all-start = ((bf16[64,128,128]{2,1,0:T(8,128)(2,1)}), bf16[64,128,128]{2,1,0:T(8,128)(2,1)}, u32[]{:S(2)}, u32[]{:S(2)}) async-start(bf16[64,128,128]{2,1,0:T(8,128)(2,1)} %stack.2), calls=%async_computation | async-start | bytes 4194304 | tf_op jit(solution)/shard_map/all_to_all | solution.py:90
  30.6 98.6 %all-to-all-done = bf16[64,128,128]{2,1,0:T(8,128)(2,1)} async-done(((bf16[64,128,128]{2,1,0:T(8,128)(2,1)}), bf16[64,128,128]{2,1,0:T(8,128)(2,1)}, u32[]{:S(2)}, u32[]{:S(2)}) %all-to-all-start) | async-done | bytes 2097184 | tf_op jit(solution)/shard_map/all_to_all | solution.py:90
  129.2 36.7 %while.36 = (s32[]{:T(128)}, f32[8,128]{1,0:T(8,128)S(1)}, f32[8,128]{1,0:T(8,128)S(1)}, s32[128]{0:T(128)S(1)}, s32[128]{0:T(128)S(1)}, /*index=5*/bf16[8192,12...) while((s32[]{:T(128)}, f32[8,128]{1,0:T(8,128)S(1)}, ...), condition=%wide.region_5.6_spmd.clone, body=%wide.region_1.5_spmd.clone.sunk | while | flops 138169856 | bytes 4850866 | solution.py:40
  165.9 25.3 %all-gather.2.cloned.1.call-done = bf16[8192,128]{0,1:T(8,128)(2,1)} async-done(((bf16[128,128]{0,1:T(8,128)(2,1)}), bf16[8192,128]{0,1:T(8,128)(2,1)}) %all-gather.2.cloned.1.call-update) | async-done | bytes 2097168 | tf_op jit(solution)/shard_map/all_gather | solution.py:92
  191.2 59.8 %while.37 = (s32[]{:T(128)}, f32[128,8,128]{0,2,1:T(8,128)S(1)}, f32[8192]{0:T(1024)S(1)}, bf16[8192,128]{0,1:T(8,128)(2,1)}, s32[128]{0:T(128)S(1)}, /*index=5*...) while((s32[]{:T(128)}, f32[128,8,128]{0,2,1:T(8,128)S(1)}, ...), condition=%wide.region_9.10_spmd.clone, body=%wide.region_6.9_spmd.clone.sunk | while | flops 271595520 | bytes 3824841 | solution.py:40
  191.6 1.6 fusion.47
  193.2 1.4 fusion.48
  195.3 1.6 fusion.47
  197.0 1.4 fusion.48
  199.1 1.6 fusion.47
  200.7 1.4 fusion.48
  202.8 1.6 fusion.47
  204.4 1.4 fusion.48
  206.6 1.6 fusion.47
  208.2 1.4 fusion.48
  210.3 1.6 fusion.47
  211.9 1.4 fusion.48
  214.0 1.6 fusion.47
  215.7 1.4 fusion.48
  217.8 1.6 fusion.47
  221.5 1.6 fusion.47
  225.3 1.6 fusion.47
  229.0 1.6 fusion.47
  232.7 1.6 fusion.47
  236.5 1.6 fusion.47
  240.2 1.6 fusion.47
  243.9 1.6 fusion.47
  245.6 1.4 fusion.48
  247.7 1.6 fusion.47
  249.3 1.4 fusion.48
  251.9 209.3 %all-reduce = f32[8192]{0:T(1024)S(1)} all-reduce(f32[8192]{0:T(1024)S(1)} %get-tuple-element.410), channel_id=2, replica_groups=mesh['seq'=64,'kv'=8] {'seq'}, use_global_device_ids=true, to_apply=%region_10.11.clone | all-reduce | flops 8192 | bytes 65536
  (256 shorter events, 60.1 us)
Async XLA Ops:
  9.8 17.6 %copy-start.2 = (bf16[128,128]{1,0:T(8,128)(2,1)S(1)}, bf16[128,128]{1,0:T(8,128)(2,1)}, u32[]{:S(2)}) copy-start(bf16[128,128]{1,0:T(8,128)(2,1)} %param.10) | copy-start | bytes 98308
  9.8 18.4 %copy-start = (bf16[128,1024]{1,0:T(8,128)(2,1)S(1)}, bf16[128,1024]{1,0:T(8,128)(2,1)}, u32[]{:S(2)}) copy-start(bf16[128,1024]{1,0:T(8,128)(2,1)} %param.8) | copy-start | bytes 786436
  9.8 20.6 %copy-start.1 = (s32[128]{0:T(128)S(1)}, s32[128]{0:T(128)}, u32[]{:S(2)}) copy-start(s32[128]{0:T(128)} %param.11) | copy-start | bytes 1540
  9.8 119.4 %all-to-all-start = ((bf16[64,128,128]{2,1,0:T(8,128)(2,1)}), bf16[64,128,128]{2,1,0:T(8,128)(2,1)}, u32[]{:S(2)}, u32[]{:S(2)}) async-start(bf16[64,128,128]{2,1,0:T(8,128)(2,1)} %stack.2), calls=%async_computation | async-start | bytes 4194304 | tf_op jit(solution)/shard_map/all_to_all | solution.py:90
  27.3 163.9 %all-gather.2.cloned.1.call-start = ((), (), s32[]{:S(2)}) async-start(), calls=%async_computation.1 | async-start | bytes 2129920 | tf_op jit(solution)/shard_map/all_gather | solution.py:92
  251.0 210.8 %copy-start.3 = (f32[8,128]{1,0:T(8,128)}, f32[8,128]{1,0:T(8,128)S(1)}, u32[]{:S(2)}) copy-start(f32[8,128]{1,0:T(8,128)S(1)} %get-tuple-element.736) | copy-start | bytes 12292
Sparse Core Ops, SparseCore 0:
  30.8 160.4 all-gather.1
